TPU v7x, 512 devices: a whole 4x4x16 slice. The times are simulated.
512 devices in a mesh: row: 16 (over z), col: 16 (over y_hi, x, core), chan: 2 (over y_lo).
Axes of the slice: x: 4, y: 4 (y_hi: 2, y_lo: 2; y = y_hi * 2 + y_lo), z: 16, core: 2. Of those that a mesh axis runs over, the one named last changes fastest.
Arguments:
- array_volts: bfloat16 [6, 2, 2048, 2048], P('chan', None, ('row', 'col')), parts along dimension 0, may hold values from -15 to 15, as said below
- reference_volts: bfloat16 [6, 2, 32, 2048], P('chan', None, None, 'col'), parts along dimension 0, may hold values from -15 to 15, as said below
Outputs:
- cleaned: float32 [6, 2, 2048, 2048], P('chan', None, 'row', 'col'), parts along dimension 0
There are 2 independent parts, one for each index of `chan`. A program takes and returns all parts, laid end to end along the dimension named above; each array names one. Nothing has to cross between parts.
Inputs may be any that keep to these rules, and one draw needn't show every extreme that they name: `array_volts`: array voltages: common interference from a few sources plus independent noise. `reference_volts`: reference voltages: the same interference sources seen with other gains, plus independent noise.
All inputs are finite; a program needn't handle non-finite values.
Results may differ from a plain program's by a relative error of at most 0.0003.
Values may be sent and summed in bfloat16 or wider, within the bound.
A program may use at most 64 MiB of HBM per device.

v0:
```python
import jax
import jax.numpy as jnp
from jax import lax
from jax.sharding import PartitionSpec as P


def in_order(blocks, dim):
    shape = list(blocks.shape[1:])
    shape[dim] *= blocks.shape[0]
    return jnp.moveaxis(blocks, 0, dim).reshape(shape)


def sent_to_all(x, axis):
    copies = jnp.broadcast_to(x, (lax.axis_size(axis), *x.shape))
    return lax.all_to_all(copies, axis, split_axis=0, concat_axis=0, tiled=True)


def collect(x, axis, dim):
    return in_order(sent_to_all(x, axis), dim)


def correlate(first_rows, second_rows):
    width_first = first_rows.shape[1]
    width_second = second_rows.shape[1]
    samples = first_rows.shape[2]
    stacked_first = first_rows.reshape(2 * width_first, samples)
    stacked_second = second_rows.reshape(2 * width_second, samples)
    product = jnp.einsum(
        "xn,yn->xy", stacked_first, stacked_second, preferred_element_type=jnp.float32
    )
    real_part = product[:width_first, :width_second] + product[width_first:, width_second:]
    imaginary_portion = product[width_first:, :width_second] - product[:width_first, width_second:]
    return jnp.stack([real_part, imaginary_portion]) / jnp.float32(samples)


def subtract(vis_tile, rows_cross, cross_cols, reference_covariance):
    real_cov = reference_covariance[0]
    imag_cov = reference_covariance[1]
    system = jnp.concatenate(
        [jnp.concatenate([real_cov, -imag_cov], 1), jnp.concatenate([imag_cov, real_cov], 1)], 0
    )
    lower_factor = jnp.linalg.cholesky(system)
    right_hand = jnp.concatenate([cross_cols[0], cross_cols[1]], 0)
    middle = lax.linalg.triangular_solve(lower_factor, right_hand, left_side=True, lower=True)
    solved = lax.linalg.triangular_solve(
        lower_factor, middle, left_side=True, lower=True, transpose_a=True
    )
    half_size = real_cov.shape[0]
    solved_real = solved[:half_size]
    solved_imag = solved[half_size:]
    highest = lax.Precision.HIGHEST
    corr_real = jnp.dot(rows_cross[0], solved_real, precision=highest) - jnp.dot(
        rows_cross[1], solved_imag, precision=highest
    )
    corr_imag = jnp.dot(rows_cross[0], solved_imag, precision=highest) + jnp.dot(
        rows_cross[1], solved_real, precision=highest
    )
    return vis_tile - jnp.stack([corr_real, corr_imag])


def per_device(array_volts, reference_volts):
    results = []
    for sub_index in range(array_volts.shape[0]):
        local_volts = array_volts[sub_index]
        ref_all = collect(reference_volts[sub_index], "col", 2)
        reference_covariance = correlate(ref_all, ref_all)
        row_volts = collect(local_volts, "col", 1)
        width_rows = row_volts.shape[1]
        left_factor_matrix = jnp.concatenate([row_volts, ref_all], 1)
        joined = correlate(
            left_factor_matrix, lax.all_gather(local_volts, "row", axis=1, tiled=True)
        )
        vis_tile = joined[:, :width_rows]
        cross_cols = joined[:, width_rows:]
        rows_cross = correlate(row_volts, ref_all)
        results.append(subtract(vis_tile, rows_cross, cross_cols, reference_covariance))
    return jnp.stack(results)


def solution(mesh):
    return jax.shard_map(
        per_device,
        mesh=mesh,
        in_specs=(P("chan", None, ("row", "col"), None), P("chan", None, None, "col")),
        out_specs=P("chan", None, "row", "col"),
        check_vma=False,
    )
```

profile of v0, /device:TPU:2, one launch (start us, length us, event | category | flops | bytes accessed | tf_op | source)
XLA Modules:
  0.0 237.6 jit_solution(3841975494435622801)
XLA Ops:
  6.5 1.6 fusion.99
  8.2 0.7 all-gather.9.cloned.1.call-update
  8.9 0.8 slice_bitcast_fusion.20
  9.7 0.8 broadcast_in_dim.24
  10.4 9.2 %all-to-all-start.5 = ((bf16[16,2,32,128]{3,2,1,0:T(8,128)(2,1)}), bf16[16,2,32,128]{3,2,1,0:T(8,128)(2,1)S(1)}, u32[]{:S(2)}, u32[]{:S(2)}) async-start(bf16[16,2,32,128]{3,2,1,0:T(8,128)(2,1)} %broadcast_in_dim.24), calls=%async_computation.5 | async-start | bytes 524288 | tf_op jit(solution)/shard_map/all_to_all | solution.py:15
  19.7 0.7 all-gather.7.cloned.1.call-update
  20.4 6.3 %all-to-all-done.5 = bf16[16,2,32,128]{3,2,1,0:T(8,128)(2,1)S(1)} async-done(((bf16[16,2,32,128]{3,2,1,0:T(8,128)(2,1)}), bf16[16,2,32,128]{3,2,1,0:T(8,128)(2,1)S(1)}, u32[]{:S(2)}, u32[]{:S(2)}) %all-to-all-start.5) | async-done | bytes 262176 | tf_op jit(solution)/shard_map/all_to_all | solution.py:15
  26.7 0.8 broadcast_in_dim.22
  27.4 5.8 %all-to-all-start.3 = ((bf16[16,2,32,128]{3,2,1,0:T(8,128)(2,1)}), bf16[16,2,32,128]{3,2,1,0:T(8,128)(2,1)S(1)}, u32[]{:S(2)}, u32[]{:S(2)}) async-start(bf16[16,2,32,128]{3,2,1,0:T(8,128)(2,1)} %broadcast_in_dim.22), calls=%async_computation.3 | async-start | bytes 524288 | tf_op jit(solution)/shard_map/all_to_all | solution.py:15
  34.2 6.1 %all-to-all-done.3 = bf16[16,2,32,128]{3,2,1,0:T(8,128)(2,1)S(1)} async-done(((bf16[16,2,32,128]{3,2,1,0:T(8,128)(2,1)}), bf16[16,2,32,128]{3,2,1,0:T(8,128)(2,1)S(1)}, u32[]{:S(2)}, u32[]{:S(2)}) %all-to-all-start.3) | async-done | bytes 262176 | tf_op jit(solution)/shard_map/all_to_all | solution.py:15
  40.3 0.8 broadcast_in_dim.20
  41.1 5.8 %all-to-all-start.1 = ((bf16[16,2,32,128]{3,2,1,0:T(8,128)(2,1)}), bf16[16,2,32,128]{3,2,1,0:T(8,128)(2,1)S(1)}, u32[]{:S(2)}, u32[]{:S(2)}) async-start(bf16[16,2,32,128]{3,2,1,0:T(8,128)(2,1)} %broadcast_in_dim.20), calls=%async_computation.1 | async-start | bytes 524288 | tf_op jit(solution)/shard_map/all_to_all | solution.py:15
  47.8 6.2 %all-to-all-done.1 = bf16[16,2,32,128]{3,2,1,0:T(8,128)(2,1)S(1)} async-done(((bf16[16,2,32,128]{3,2,1,0:T(8,128)(2,1)}), bf16[16,2,32,128]{3,2,1,0:T(8,128)(2,1)S(1)}, u32[]{:S(2)}, u32[]{:S(2)}) %all-to-all-start.1) | async-done | bytes 262176 | tf_op jit(solution)/shard_map/all_to_all | solution.py:15
  54.0 1.1 broadcast_in_dim.23
  55.1 6.0 %all-to-all-start.4 = ((bf16[16,2,8,2048]{3,2,1,0:T(8,128)(2,1)}), bf16[16,2,8,2048]{3,2,1,0:T(8,128)(2,1)S(1)}, u32[]{:S(2)}, u32[]{:S(2)}) async-start(bf16[16,2,8,2048]{3,2,1,0:T(8,128)(2,1)} %broadcast_in_dim.23), calls=%async_computation.4 | async-start | bytes 2097152 | tf_op jit(solution)/shard_map/all_to_all | solution.py:15
  61.2 0.7 copy-done.6
  62.5 5.9 %cholesky.81 = f32[64,64]{1,0:T(8,128)S(1)} custom-call(f32[64,64]{1,0:T(8,128)S(1)} %fusion.51), custom_call_target="Cholesky" | custom-call | tf_op jit(solution)/shard_map/jit(cholesky)/cholesky | solution.py:42
  68.4 0.7 compare_reduce_fusion
  69.3 5.9 %cholesky.70 = f32[64,64]{1,0:T(8,128)S(1)} custom-call(f32[64,64]{1,0:T(8,128)S(1)} %fusion.55), custom_call_target="Cholesky" | custom-call | tf_op jit(solution)/shard_map/jit(cholesky)/cholesky | solution.py:42
  75.5 5.9 %cholesky.59 = f32[64,64]{1,0:T(8,128)S(1)} custom-call(f32[64,64]{1,0:T(8,128)S(1)} %fusion.59), custom_call_target="Cholesky" | custom-call | tf_op jit(solution)/shard_map/jit(cholesky)/cholesky | solution.py:42
  81.3 0.7 compare_reduce_fusion.1
  82.1 0.6 fusion.35
  82.7 0.6 fusion.34
  83.4 1.1 broadcast_in_dim.21
  84.5 7.3 %all-to-all-start.2 = ((bf16[16,2,8,2048]{3,2,1,0:T(8,128)(2,1)}), bf16[16,2,8,2048]{3,2,1,0:T(8,128)(2,1)S(1)}, u32[]{:S(2)}, u32[]{:S(2)}) async-start(bf16[16,2,8,2048]{3,2,1,0:T(8,128)(2,1)} %broadcast_in_dim.21), calls=%async_computation.2 | async-start | bytes 2097152 | tf_op jit(solution)/shard_map/all_to_all | solution.py:15
  91.8 0.7 compare_reduce_fusion.2
  92.4 0.7 copy_bitcast_fusion.1
  93.2 0.7 copy_bitcast_fusion.2
  93.9 12.8 %all-to-all-done.2 = bf16[16,2,8,2048]{3,2,1,0:T(8,128)(2,1)S(1)} async-done(((bf16[16,2,8,2048]{3,2,1,0:T(8,128)(2,1)}), bf16[16,2,8,2048]{3,2,1,0:T(8,128)(2,1)S(1)}, u32[]{:S(2)}, u32[]{:S(2)}) %all-to-all-start.2) | async-done | bytes 1048608 | tf_op jit(solution)/shard_map/all_to_all | solution.py:15
  106.7 1.1 broadcast_in_dim.19
  107.8 7.2 %all-to-all-start = ((bf16[16,2,8,2048]{3,2,1,0:T(8,128)(2,1)}), bf16[16,2,8,2048]{3,2,1,0:T(8,128)(2,1)}, u32[]{:S(2)}, u32[]{:S(2)}) async-start(bf16[16,2,8,2048]{3,2,1,0:T(8,128)(2,1)} %broadcast_in_dim.19), calls=%async_computation | async-start | bytes 2097152 | tf_op jit(solution)/shard_map/all_to_all | solution.py:15
  115.0 0.6 fusion.33
  115.7 4.9 %custom-call.17 = f32[1,64,64]{1,2,0:T(8,128)S(1)} custom-call(f32[1,64,64]{2,1,0:T(8,128)S(1)} %fusion.35), custom_call_target="InvertDiagBlocksLowerTriangular" | custom-call | tf_op jit(solution)/shard_map/triangular_solve/custom-call.2 | solution.py:45
  120.6 4.9 %custom-call.15 = f32[1,64,64]{1,2,0:T(8,128)S(1)} custom-call(f32[1,64,64]{2,1,0:T(8,128)S(1)} %fusion.34), custom_call_target="InvertDiagBlocksLowerTriangular" | custom-call | tf_op jit(solution)/shard_map/triangular_solve/custom-call.2 | solution.py:45
  125.5 4.9 %custom-call.13 = f32[1,64,64]{1,2,0:T(8,128)S(1)} custom-call(f32[1,64,64]{2,1,0:T(8,128)S(1)} %fusion.33), custom_call_target="InvertDiagBlocksLowerTriangular" | custom-call | tf_op jit(solution)/shard_map/triangular_solve/custom-call.2 | solution.py:45
  130.7 0.8 copy-done.3
  131.5 0.4 fusion.8
  132.0 0.4 fusion.12
  132.4 1.3 copy.120
  133.8 0.4 fusion.16
  134.3 1.2 pad_maximum_fusion.2
  135.6 0.8 copy-done
  136.5 2.2 fusion.102
  138.8 16.9 %all-gather.9.cloned.1.call-done = bf16[1,2,128,2048]{3,2,1,0:T(8,128)(2,1)} async-done(((bf16[1,2,8,2048]{3,2,1,0:T(8,128)(2,1)}), bf16[1,2,128,2048]{3,2,1,0:T(8,128)(2,1)}) %all-gather.9.cloned.1.call-update) | async-done | bytes 1048592 | tf_op jit(solution)/shard_map/all_gather | solution.py:71
  155.7 1.8 fusion.101
  159.5 66.1 %all-gather.7.cloned.1.call-done = bf16[1,2,128,2048]{3,2,1,0:T(8,128)(2,1)} async-done(((bf16[1,2,8,2048]{3,2,1,0:T(8,128)(2,1)}), bf16[1,2,128,2048]{3,2,1,0:T(8,128)(2,1)}) %all-gather.7.cloned.1.call-update) | async-done | bytes 1048592 | tf_op jit(solution)/shard_map/all_gather | solution.py:71
  225.6 1.8 fusion.100
  230.3 0.8 pad_maximum_fusion.3
  (90 shorter events, 8.4 us)
Async XLA Ops:
  6.5 130.0 %all-gather.11.cloned.1.call-start = ((), (), s32[]{:S(2)}) async-start(), calls=%async_computation.8 | async-start | bytes 1114112 | tf_op jit(solution)/shard_map/all_gather | solution.py:71
  8.2 147.5 %all-gather.9.cloned.1.call-start = ((), (), s32[]{:S(2)}) async-start(), calls=%async_computation.7 | async-start | bytes 1114112 | tf_op jit(solution)/shard_map/all_gather | solution.py:71
  10.4 16.3 %all-to-all-start.5 = ((bf16[16,2,32,128]{3,2,1,0:T(8,128)(2,1)}), bf16[16,2,32,128]{3,2,1,0:T(8,128)(2,1)S(1)}, u32[]{:S(2)}, u32[]{:S(2)}) async-start(bf16[16,2,32,128]{3,2,1,0:T(8,128)(2,1)} %broadcast_in_dim.24), calls=%async_computation.5 | async-start | bytes 524288 | tf_op jit(solution)/shard_map/all_to_all | solution.py:15
  19.7 206.0 %all-gather.7.cloned.1.call-start = ((), (), s32[]{:S(2)}) async-start(), calls=%async_computation.6 | async-start | bytes 1114112 | tf_op jit(solution)/shard_map/all_gather | solution.py:71
  27.4 12.9 %all-to-all-start.3 = ((bf16[16,2,32,128]{3,2,1,0:T(8,128)(2,1)}), bf16[16,2,32,128]{3,2,1,0:T(8,128)(2,1)S(1)}, u32[]{:S(2)}, u32[]{:S(2)}) async-start(bf16[16,2,32,128]{3,2,1,0:T(8,128)(2,1)} %broadcast_in_dim.22), calls=%async_computation.3 | async-start | bytes 524288 | tf_op jit(solution)/shard_map/all_to_all | solution.py:15
  33.5 0.7 copy-start.2
  41.1 12.9 %all-to-all-start.1 = ((bf16[16,2,32,128]{3,2,1,0:T(8,128)(2,1)}), bf16[16,2,32,128]{3,2,1,0:T(8,128)(2,1)S(1)}, u32[]{:S(2)}, u32[]{:S(2)}) async-start(bf16[16,2,32,128]{3,2,1,0:T(8,128)(2,1)} %broadcast_in_dim.20), calls=%async_computation.1 | async-start | bytes 524288 | tf_op jit(solution)/shard_map/all_to_all | solution.py:15
  47.1 0.7 copy-start.4
  55.1 28.3 %all-to-all-start.4 = ((bf16[16,2,8,2048]{3,2,1,0:T(8,128)(2,1)}), bf16[16,2,8,2048]{3,2,1,0:T(8,128)(2,1)S(1)}, u32[]{:S(2)}, u32[]{:S(2)}) async-start(bf16[16,2,8,2048]{3,2,1,0:T(8,128)(2,1)} %broadcast_in_dim.23), calls=%async_computation.4 | async-start | bytes 2097152 | tf_op jit(solution)/shard_map/all_to_all | solution.py:15
  61.2 0.7 copy-start.6
  84.5 22.2 %all-to-all-start.2 = ((bf16[16,2,8,2048]{3,2,1,0:T(8,128)(2,1)}), bf16[16,2,8,2048]{3,2,1,0:T(8,128)(2,1)S(1)}, u32[]{:S(2)}, u32[]{:S(2)}) async-start(bf16[16,2,8,2048]{3,2,1,0:T(8,128)(2,1)} %broadcast_in_dim.21), calls=%async_computation.2 | async-start | bytes 2097152 | tf_op jit(solution)/shard_map/all_to_all | solution.py:15
  107.8 24.6 %all-to-all-start = ((bf16[16,2,8,2048]{3,2,1,0:T(8,128)(2,1)}), bf16[16,2,8,2048]{3,2,1,0:T(8,128)(2,1)}, u32[]{:S(2)}, u32[]{:S(2)}) async-start(bf16[16,2,8,2048]{3,2,1,0:T(8,128)(2,1)} %broadcast_in_dim.19), calls=%async_computation | async-start | bytes 2097152 | tf_op jit(solution)/shard_map/all_to_all | solution.py:15
  130.5 1.0 copy-start.3
  130.6 1.4 copy-start.5
  132.4 1.4 copy-start.7
  134.2 1.2 copy-start.1
  135.4 1.0 copy-start
Sparse Core Ops, SparseCore 0:
  9.4 75.7 all-gather.10
  87.4 68.2 all-gather.8
  157.8 67.7 all-gather.6
where the time goes:
time: 239 us; the launch traced here: 238 us
  waiting for transfers between devices  116 us (49%)
  starting transfers between devices  41.5 us (17%)
  other arithmetic  39.4 us (16%)
  local copies, waits for them, and re-layouts  14.8 us (6%)
  between operations  13.7 us (6%)
  matrix products  12.3 us (5%)
    all_gather x3, waiting for transfers between devices, per_device(): lax.all_gather(local_volts, 'row', axis=1, tiled=True)  83.1 us
    all_to_all x6, starting transfers between devices, sent_to_all(): return lax.all_to_all(copies, axis, split_axis=0, concat_axis=0, tiled=True)  41.4 us
    all_to_all x6, waiting for transfers between devices, sent_to_all(): return lax.all_to_all(copies, axis, split_axis=0, concat_axis=0, tiled=True)  31.4 us
    another operation x9, other arithmetic, subtract(): lower_factor = jnp.linalg.cholesky(system)  19.7 us
    another operation x6, other arithmetic, subtract(): lax.linalg.triangular_solve(lower_factor, middle, left_side=True, lower=T...  16.6 us
    dot_general x9, matrix products, correlate(): jnp.einsum('xn,yn->xy', stacked_first, stacked_second, preferred_element_...  7.67 us
    broadcast_in_dim x6, local copies, waits for them, and re-layouts, sent_to_all(): copies = jnp.broadcast_to(x, (lax.axis_size(axis), *x.shape))  5.59 us
  transfers between devices with their start and end apart: 9, of which 6 were waited for; matrix products, arithmetic and copies ran while one was open for 24% of the time, Pallas kernels for 0%

commit v1 on v0

--- a/solution.py
+++ b/solution.py
@@ -1,7 +1,23 @@
+import functools
 import jax
 import jax.numpy as jnp
 from jax import lax
 from jax.sharding import PartitionSpec as P
+
+
+def report_edge(local, shard_axis):
+    return jnp.concatenate(
+        jax.lax.all_to_all(
+            jnp.stack([local] * jax.lax.axis_size(shard_axis)),
+            axis_name=shard_axis,
+            split_axis=0,
+            concat_axis=0,
+        ),
+        axis=1,
+    )
+
+
+_recast_types = functools.partial(report_edge, shard_axis="row")
 
 
 def in_order(blocks, dim):
@@ -67,9 +83,7 @@
         row_volts = collect(local_volts, "col", 1)
         width_rows = row_volts.shape[1]
         left_factor_matrix = jnp.concatenate([row_volts, ref_all], 1)
-        joined = correlate(
-            left_factor_matrix, lax.all_gather(local_volts, "row", axis=1, tiled=True)
-        )
+        joined = correlate(left_factor_matrix, _recast_types(local_volts))
         vis_tile = joined[:, :width_rows]
         cross_cols = joined[:, width_rows:]
         rows_cross = correlate(row_volts, ref_all)

time: 239 us -> 301 us (1.26)
  the two profiles are of different devices: /device:TPU:2 before, /device:TPU:32 now
where the time goes in v1:
time: 301 us; the launch traced here: 300 us
  waiting for transfers between devices  112 us (37%)
  blocking collectives  72 us (24%)
  other arithmetic  47.3 us (16%)
  starting transfers between devices  40.1 us (13%)
  local copies, waits for them, and re-layouts  19 us (6%)
  matrix products  8.22 us (3%)
    all_to_all x3, waiting for transfers between devices, report_edge(): jax.lax.all_to_all(jnp.stack([local] * jax.lax.axis_size(shard_axis)), ax...  86 us
    all_to_all x4, blocking collectives, sent_to_all(): return lax.all_to_all(copies, axis, split_axis=0, concat_axis=0, tiled=True)  72 us
    all_to_all x3, starting transfers between devices, report_edge(): jax.lax.all_to_all(jnp.stack([local] * jax.lax.axis_size(shard_axis)), ax...  32.3 us
    all_to_all x2, waiting for transfers between devices, sent_to_all(): return lax.all_to_all(copies, axis, split_axis=0, concat_axis=0, tiled=True)  26.4 us
    another operation x6, other arithmetic, subtract(): lax.linalg.triangular_solve(lower_factor, middle, left_side=True, lower=T...  20.5 us
    another operation x9, other arithmetic, subtract(): lower_factor = jnp.linalg.cholesky(system)  20.4 us
    all_to_all x2, starting transfers between devices, sent_to_all(): return lax.all_to_all(copies, axis, split_axis=0, concat_axis=0, tiled=True)  7.85 us
  transfers between devices with their start and end apart: 5, of which 5 were waited for; matrix products, arithmetic and copies ran while one was open for 20% of the time, Pallas kernels for 0%

profile of v1, /device:TPU:32, one launch (start us, length us, event | category | flops | bytes accessed | tf_op | source)
XLA Modules:
  0.0 299.7 jit_solution(1724184283934996901)
XLA Ops:
  0.0 0.8 slice_bitcast_fusion.23
  0.8 16.2 %all_to_all.45 = bf16[16,2,32,128]{3,2,1,0:T(8,128)(2,1)S(1)} all-to-all(bf16[16,2,32,128]{3,2,1,0:T(8,128)(2,1)S(1)} %broadcast_in_dim.20), channel_id=1, replica_groups=mesh['row'=16,'col'=16,'chan'=2] {'col'}, dimensions={0} | all-to-all | bytes 524288 | tf_op jit(solution)/shard_map/all_to_all | solution.py:31
  17.1 12.7 %all_to_all.46 = bf16[16,2,32,128]{3,2,1,0:T(8,128)(2,1)} all-to-all(bf16[16,2,32,128]{3,2,1,0:T(8,128)(2,1)S(1)} %broadcast_in_dim.24), channel_id=1, replica_groups=mesh['row'=16,'col'=16,'chan'=2] {'col'}, dimensions={0} | all-to-all | bytes 524288 | tf_op jit(solution)/shard_map/all_to_all | solution.py:31
  29.8 0.8 broadcast_in_dim.22
  30.5 4.2 %all-to-all-start.4 = ((bf16[16,2,32,128]{3,2,1,0:T(8,128)(2,1)}), bf16[16,2,32,128]{3,2,1,0:T(8,128)(2,1)}, u32[]{:S(2)}, u32[]{:S(2)}) async-start(bf16[16,2,32,128]{3,2,1,0:T(8,128)(2,1)} %broadcast_in_dim.22), calls=%async_computation.4 | async-start | bytes 524288 | tf_op jit(solution)/shard_map/all_to_all | solution.py:31
  34.8 9.4 %all-to-all-done.4 = bf16[16,2,32,128]{3,2,1,0:T(8,128)(2,1)} async-done(((bf16[16,2,32,128]{3,2,1,0:T(8,128)(2,1)}), bf16[16,2,32,128]{3,2,1,0:T(8,128)(2,1)}, u32[]{:S(2)}, u32[]{:S(2)}) %all-to-all-start.4) | async-done | bytes 262176 | tf_op jit(solution)/shard_map/all_to_all | solution.py:31
  44.1 1.1 broadcast_in_dim.19
  45.2 21.6 %all_to_all.47 = bf16[16,2,8,2048]{3,2,1,0:T(8,128)(2,1)S(1)} all-to-all(bf16[16,2,8,2048]{3,2,1,0:T(8,128)(2,1)} %broadcast_in_dim.19), channel_id=1, replica_groups=mesh['row'=16,'col'=16,'chan'=2] {'col'}, dimensions={0} | all-to-all | bytes 2097152 | tf_op jit(solution)/shard_map/all_to_all | solution.py:31
  66.8 1.1 broadcast_in_dim.23
  67.9 21.6 %all_to_all.48 = bf16[16,2,8,2048]{3,2,1,0:T(8,128)(2,1)S(1)} all-to-all(bf16[16,2,8,2048]{3,2,1,0:T(8,128)(2,1)} %broadcast_in_dim.23), channel_id=1, replica_groups=mesh['row'=16,'col'=16,'chan'=2] {'col'}, dimensions={0} | all-to-all | bytes 2097152 | tf_op jit(solution)/shard_map/all_to_all | solution.py:31
  89.5 1.1 broadcast_in_dim.21
  90.6 3.7 %all-to-all-start.3 = ((bf16[16,2,8,2048]{3,2,1,0:T(8,128)(2,1)}), bf16[16,2,8,2048]{3,2,1,0:T(8,128)(2,1)S(1)}, u32[]{:S(2)}, u32[]{:S(2)}) async-start(bf16[16,2,8,2048]{3,2,1,0:T(8,128)(2,1)} %broadcast_in_dim.21), calls=%async_computation.3 | async-start | bytes 2097152 | tf_op jit(solution)/shard_map/all_to_all | solution.py:31
  95.1 17.1 %all-to-all-done.3 = bf16[16,2,8,2048]{3,2,1,0:T(8,128)(2,1)S(1)} async-done(((bf16[16,2,8,2048]{3,2,1,0:T(8,128)(2,1)}), bf16[16,2,8,2048]{3,2,1,0:T(8,128)(2,1)S(1)}, u32[]{:S(2)}, u32[]{:S(2)}) %all-to-all-start.3) | async-done | bytes 1048608 | tf_op jit(solution)/shard_map/all_to_all | solution.py:31
  112.2 1.0 copy-done.2
  113.2 15.2 %all-to-all-start.2 = ((bf16[16,2,8,2048]{3,2,1,0:T(8,128)(2,1)}), bf16[16,2,8,2048]{3,2,1,0:T(8,128)(2,1)S(1)}, u32[]{:S(2)}, u32[]{:S(2)}) async-start(bf16[16,2,8,2048]{3,2,1,0:T(8,128)(2,1)} %broadcast_in_dim.19), calls=%async_computation.2 | async-start | bytes 2097152 | tf_op jit(solution)/shard_map/all_to_all | solution.py:10
  128.6 5.9 %cholesky.59 = f32[64,64]{1,0:T(8,128)S(1)} custom-call(f32[64,64]{1,0:T(8,128)S(1)} %fusion.59), custom_call_target="Cholesky" | custom-call | tf_op jit(solution)/shard_map/jit(cholesky)/cholesky | solution.py:58
  134.5 1.1 copy.76
  136.1 0.7 fusion.51
  136.8 6.6 %cholesky.81 = f32[64,64]{1,0:T(8,128)S(1)} custom-call(f32[64,64]{1,0:T(8,128)} %fusion.51), custom_call_target="Cholesky" | custom-call | tf_op jit(solution)/shard_map/jit(cholesky)/cholesky | solution.py:58
  143.4 1.1 copy.67
  145.3 0.7 maximum_maximum_fusion.1
  146.0 0.9 copy.74
  146.9 0.7 compare_reduce_fusion.2
  147.6 0.7 compare_reduce_fusion
  148.3 1.2 fusion.33
  149.5 1.2 fusion.35
  150.7 26.8 %all-to-all-done.2 = bf16[16,2,8,2048]{3,2,1,0:T(8,128)(2,1)S(1)} async-done(((bf16[16,2,8,2048]{3,2,1,0:T(8,128)(2,1)}), bf16[16,2,8,2048]{3,2,1,0:T(8,128)(2,1)S(1)}, u32[]{:S(2)}, u32[]{:S(2)}) %all-to-all-start.2) | async-done | bytes 1048608 | tf_op jit(solution)/shard_map/all_to_all | solution.py:10
  177.5 8.7 %all-to-all-start.8 = ((bf16[16,2,8,2048]{3,2,1,0:T(8,128)(2,1)}), bf16[16,2,8,2048]{3,2,1,0:T(8,128)(2,1)}, u32[]{:S(2)}, u32[]{:S(2)}) async-start(bf16[16,2,8,2048]{3,2,1,0:T(8,128)(2,1)} %broadcast_in_dim.23), calls=%async_computation.8 | async-start | bytes 2097152 | tf_op jit(solution)/shard_map/all_to_all | solution.py:10
  186.3 6.3 %custom-call.13 = f32[1,64,64]{1,2,0:T(8,128)} custom-call(f32[1,64,64]{2,1,0:T(8,128)} %fusion.33), custom_call_target="InvertDiagBlocksLowerTriangular" | custom-call | tf_op jit(solution)/shard_map/triangular_solve/custom-call.2 | solution.py:61
  192.6 6.3 %custom-call.17 = f32[1,64,64]{1,2,0:T(8,128)} custom-call(f32[1,64,64]{2,1,0:T(8,128)} %fusion.35), custom_call_target="InvertDiagBlocksLowerTriangular" | custom-call | tf_op jit(solution)/shard_map/triangular_solve/custom-call.2 | solution.py:61
  198.8 5.8 %cholesky.70 = f32[64,64]{1,0:T(8,128)S(1)} custom-call(f32[64,64]{1,0:T(8,128)S(1)} %fusion.55), custom_call_target="Cholesky" | custom-call | tf_op jit(solution)/shard_map/jit(cholesky)/cholesky | solution.py:58
  204.7 0.7 compare_reduce_fusion.1
  205.4 0.6 fusion.34
  206.0 4.9 %custom-call.15 = f32[1,64,64]{1,2,0:T(8,128)S(1)} custom-call(f32[1,64,64]{2,1,0:T(8,128)S(1)} %fusion.34), custom_call_target="InvertDiagBlocksLowerTriangular" | custom-call | tf_op jit(solution)/shard_map/triangular_solve/custom-call.2 | solution.py:61
  211.0 1.0 copy_bitcast_fusion
  212.0 1.7 copy_bitcast_fusion.1
  213.8 1.1 copy-done.3
  215.1 0.8 copy-done.7
  217.3 1.1 pad_maximum_fusion
  218.5 1.2 pad_maximum_fusion.2
  219.6 16.4 %all-to-all-done.8 = bf16[16,2,8,2048]{3,2,1,0:T(8,128)(2,1)} async-done(((bf16[16,2,8,2048]{3,2,1,0:T(8,128)(2,1)}), bf16[16,2,8,2048]{3,2,1,0:T(8,128)(2,1)}, u32[]{:S(2)}, u32[]{:S(2)}) %all-to-all-start.8) | async-done | bytes 1048608 | tf_op jit(solution)/shard_map/all_to_all | solution.py:10
  236.0 8.4 %all-to-all-start.5 = ((bf16[16,2,8,2048]{3,2,1,0:T(8,128)(2,1)}), bf16[16,2,8,2048]{3,2,1,0:T(8,128)(2,1)}, u32[]{:S(2)}, u32[]{:S(2)}) async-start(bf16[16,2,8,2048]{3,2,1,0:T(8,128)(2,1)} %broadcast_in_dim.21), calls=%async_computation.5 | async-start | bytes 2097152 | tf_op jit(solution)/shard_map/all_to_all | solution.py:10
  244.4 1.1 pad_maximum_fusion.1
  245.6 1.4 copy.77
  247.8 0.7 copy-done
  251.3 42.8 %all-to-all-done.5 = bf16[16,2,8,2048]{3,2,1,0:T(8,128)(2,1)} async-done(((bf16[16,2,8,2048]{3,2,1,0:T(8,128)(2,1)}), bf16[16,2,8,2048]{3,2,1,0:T(8,128)(2,1)}, u32[]{:S(2)}, u32[]{:S(2)}) %all-to-all-start.5) | async-done | bytes 1048608 | tf_op jit(solution)/shard_map/all_to_all | solution.py:10
  294.1 1.3 copy.68
  298.9 0.8 pad_maximum_fusion.3
  (100 shorter events, 11.1 us)
Async XLA Ops:
  0.0 34.7 %copy-start.12 = (bf16[3,2,8,2048]{3,2,1,0:T(8,128)(2,1)S(1)}, bf16[3,2,8,2048]{3,2,1,0:T(8,128)(2,1)}, u32[]{:S(2)}) copy-start(bf16[3,2,8,2048]{3,2,1,0:T(8,128)(2,1)} %param.7) | copy-start | bytes 589828
  17.1 77.2 %copy-start.4 = (bf16[16,2,32,128]{3,2,1,0:T(8,128)(2,1)}, bf16[16,2,32,128]{3,2,1,0:T(8,128)(2,1)S(1)}, u32[]{:S(2)}) copy-start(bf16[16,2,32,128]{3,2,1,0:T(8,128)(2,1)S(1)} %all_to_all.45) | copy-start | bytes 786436
  30.5 13.6 %all-to-all-start.4 = ((bf16[16,2,32,128]{3,2,1,0:T(8,128)(2,1)}), bf16[16,2,32,128]{3,2,1,0:T(8,128)(2,1)}, u32[]{:S(2)}, u32[]{:S(2)}) async-start(bf16[16,2,32,128]{3,2,1,0:T(8,128)(2,1)} %broadcast_in_dim.22), calls=%async_computation.4 | async-start | bytes 524288 | tf_op jit(solution)/shard_map/all_to_all | solution.py:31
  90.6 21.6 %all-to-all-start.3 = ((bf16[16,2,8,2048]{3,2,1,0:T(8,128)(2,1)}), bf16[16,2,8,2048]{3,2,1,0:T(8,128)(2,1)S(1)}, u32[]{:S(2)}, u32[]{:S(2)}) async-start(bf16[16,2,8,2048]{3,2,1,0:T(8,128)(2,1)} %broadcast_in_dim.21), calls=%async_computation.3 | async-start | bytes 2097152 | tf_op jit(solution)/shard_map/all_to_all | solution.py:31
  94.4 0.7 copy-start.6
  112.2 1.0 copy-start.2
  113.2 64.4 %all-to-all-start.2 = ((bf16[16,2,8,2048]{3,2,1,0:T(8,128)(2,1)}), bf16[16,2,8,2048]{3,2,1,0:T(8,128)(2,1)S(1)}, u32[]{:S(2)}, u32[]{:S(2)}) async-start(bf16[16,2,8,2048]{3,2,1,0:T(8,128)(2,1)} %broadcast_in_dim.19), calls=%async_computation.2 | async-start | bytes 2097152 | tf_op jit(solution)/shard_map/all_to_all | solution.py:10
  135.6 9.3 %copy-start.8 = (bf16[2,32,16,128]{3,2,1,0:T(8,128)(2,1)}, bf16[2,32,16,128]{3,2,1,0:T(8,128)(2,1)S(1)}, u32[]{:S(2)}) copy-start(bf16[2,32,16,128]{3,2,1,0:T(8,128)(2,1)S(1)} %copy.76) | copy-start | bytes 786436
  144.6 0.7 copy-start.10
  146.0 65.0 %copy-start.5 = (bf16[16,2,32,128]{3,2,1,0:T(8,128)(2,1)S(1)}, bf16[16,2,32,128]{3,2,1,0:T(8,128)(2,1)}, u32[]{:S(2)}) copy-start(bf16[16,2,32,128]{3,2,1,0:T(8,128)(2,1)} %copy-done.4) | copy-start | bytes 786436
  177.5 58.4 %all-to-all-start.8 = ((bf16[16,2,8,2048]{3,2,1,0:T(8,128)(2,1)}), bf16[16,2,8,2048]{3,2,1,0:T(8,128)(2,1)}, u32[]{:S(2)}, u32[]{:S(2)}) async-start(bf16[16,2,8,2048]{3,2,1,0:T(8,128)(2,1)} %broadcast_in_dim.23), calls=%async_computation.8 | async-start | bytes 2097152 | tf_op jit(solution)/shard_map/all_to_all | solution.py:10
  213.7 1.2 copy-start.3
  214.9 0.9 copy-start.7
  215.0 1.4 copy-start.9
  215.9 1.0 copy-start.11
  236.0 58.2 %all-to-all-start.5 = ((bf16[16,2,8,2048]{3,2,1,0:T(8,128)(2,1)}), bf16[16,2,8,2048]{3,2,1,0:T(8,128)(2,1)}, u32[]{:S(2)}, u32[]{:S(2)}) async-start(bf16[16,2,8,2048]{3,2,1,0:T(8,128)(2,1)} %broadcast_in_dim.21), calls=%async_computation.5 | async-start | bytes 2097152 | tf_op jit(solution)/shard_map/all_to_all | solution.py:10
  245.6 1.6 copy-start.1
  247.2 1.3 copy-start
  248.5 0.8 copy-start.14
  248.5 1.0 copy-start.13
